TPU v7x, 32 devices: a whole 2x2x4 slice. The times are simulated.
32 devices in a mesh: tm: 4 (over x, core), coef: 8 (over z, y).
Axes of the slice: x: 2, y: 2, z: 4, core: 2. Of those that a mesh axis runs over, the one named last changes fastest.
Arguments:
- design: float32 [2048, 40960], P('tm', 'coef'), may hold values from -4 to 4
- whitening: float32 [2048, 256], P('tm'), may hold values from -1 to 3, as said below
- solution: float32 [40960, 64], P('coef'), may hold values from -6 to 6
- direction: float32 [40960, 64], P('coef'), may hold values from -6 to 6
- gradient_prev: float32 [40960, 64], P('coef'), may hold values from -25 to 25
- residual: float32 [2048, 64], P('tm'), may hold values from -6 to 6
Outputs:
- new_solution: float32 [40960, 64], P('coef')
- new_residual: float32 [2048, 64], P('tm')
- new_direction: float32 [40960, 64], P('coef')
Inputs may be any that keep to these rules, and one draw needn't show every extreme that they name: `whitening`: the first tap of every row is positive.
All inputs are finite; a program needn't handle non-finite values.
Results may differ from a plain program's by a relative error of at most 0.00008.
Values sent between devices are 32-bit elements; how exact they have to be, the bound alone decides.
A program may use at most 64 MiB of HBM per device.

v0:
```python
import jax
import jax.numpy as jnp
from jax import lax
from jax.sharding import PartitionSpec as P


def shifted(array, axis, by):
    devices = lax.axis_size(axis)
    pairs = [(i, i + by) for i in range(devices) if 0 <= i + by < devices]
    return lax.ppermute(array, axis, pairs)


def skewed_band(whitening):
    count, width = whitening.shape
    flipped = whitening[:, ::-1]
    padded = jnp.concatenate([flipped, jnp.zeros((count, count), whitening.dtype)], axis=1)
    return padded.reshape(-1)[: count * (count + width - 1)].reshape(count, count + width - 1)


def band_blocks(whitening):
    count, width = whitening.shape
    nblocks = count // width
    skewed = jax.vmap(skewed_band)(whitening.reshape(nblocks, width, width))
    return jnp.concatenate([skewed, jnp.zeros((nblocks, width, 1), jnp.float32)], axis=2)


def band_apply(blocks_band, extended):
    nblocks, width = (blocks_band.shape[0], blocks_band.shape[1])
    columns = extended.shape[1]
    padded = jnp.concatenate([extended, jnp.zeros((1, columns), jnp.float32)], axis=0)
    stacked = padded.reshape(nblocks + 1, width, columns)
    windows = jnp.concatenate([stacked[:-1], stacked[1:]], axis=1)
    result = jnp.einsum(
        "brj,bjc->brc",
        blocks_band,
        windows,
        precision=lax.Precision.HIGHEST,
        preferred_element_type=jnp.float32,
    )
    return result.reshape(nblocks * width, columns)


def band_adjoint(blocks_band, values):
    nblocks, width = (blocks_band.shape[0], blocks_band.shape[1])
    columns = values.shape[1]
    pieces = jnp.einsum(
        "brj,brc->bjc",
        blocks_band,
        values.reshape(nblocks, width, columns),
        precision=lax.Precision.HIGHEST,
        preferred_element_type=jnp.float32,
    )
    zero_block = jnp.zeros((1, width, columns), jnp.float32)
    total = jnp.concatenate([pieces[:, :width], zero_block], axis=0) + jnp.concatenate(
        [zero_block, pieces[:, width:]], axis=0
    )
    return total.reshape(-1, columns)[: nblocks * width + width - 1]


def product(left, right):
    return jnp.dot(left, right, precision=lax.Precision.HIGHEST, preferred_element_type=jnp.float32)


def product_left_t(left, right):
    return lax.dot_general(
        left,
        right,
        (((0,), (0,)), ((), ())),
        precision=lax.Precision.HIGHEST,
        preferred_element_type=jnp.float32,
    )


def per_device(design, whitening, solution, direction, gradient_prev, residual):
    count, width = whitening.shape
    rim_rows = width - 1
    banded = band_blocks(whitening)
    old_part = jnp.sum(gradient_prev * gradient_prev, axis=0)
    partial_value = product(design, direction)
    totals, old_norm = lax.psum((partial_value, old_part), "coef")
    pred_edge = shifted(totals[count - rim_rows :], "tm", 1)
    predicted = band_apply(banded, jnp.concatenate([pred_edge, totals], axis=0))
    energy = lax.psum(jnp.sum(predicted * predicted, axis=0), "tm")
    step_size = old_norm / energy
    new_solution = solution + step_size * direction
    new_residual = residual - step_size * predicted
    spread = band_adjoint(banded, new_residual)
    carried = shifted(spread[:rim_rows], "tm", -1)
    filler = jnp.zeros((count - rim_rows, spread.shape[1]), jnp.float32)
    whitened = spread[rim_rows:] + jnp.concatenate([filler, carried], axis=0)
    grad_part = product_left_t(design, whitened)
    gradient = lax.psum(grad_part, "tm")
    new_norm = lax.psum(jnp.sum(gradient * gradient, axis=0), "coef")
    new_direction = gradient + new_norm / old_norm * direction
    return (new_solution, new_residual, new_direction)


def solution(mesh):
    return jax.shard_map(
        per_device,
        mesh=mesh,
        in_specs=(
            P("tm", "coef"),
            P("tm", None),
            P("coef", None),
            P("coef", None),
            P("coef", None),
            P("tm", None),
        ),
        out_specs=(P("coef", None), P("tm", None), P("coef", None)),
        check_vma=False,
    )
```

profile of v0, /device:TPU:0, one launch (start us, length us, event | category | flops | bytes accessed | tf_op | source)
XLA Modules:
  0.0 209.4 jit_solution(6699002919569478250)
XLA Ops:
  7.2 0.0 all-reduce.9.cloned.1.call-start
  7.2 13.2 %fusion.15 = f32[512,64]{0,1:T(8,128)} fusion(f32[512,5120]{1,0:T(8,128)} %param.6, f32[5120,64]{0,1:T(8,128)} %param.9), kind=kOutput, calls=%fused_computation.29 | convolution fusion | flops 2013265920 | bytes 11927552 | tf_op jit(solution)/shard_map/dot_general | solution.py:61
  20.4 0.0 all-reduce.9.cloned.1.call-update
  20.4 0.0 all-reduce.11.cloned.1.call-start
  20.5 0.7 rev.3
  21.2 0.0 copy-done.2
  21.2 0.2 multiply_reduce_fusion.1
  21.4 71.5 %all-reduce.9.cloned.1.call-done = f32[512,64]{0,1:T(8,128)} async-done(((f32[512,64]{0,1:T(8,128)}), f32[512,64]{0,1:T(8,128)}) %all-reduce.9.cloned.1.call-update) | async-done | bytes 131088 | tf_op jit(solution)/shard_map/psum | solution.py:80
  92.9 0.9 slice.46
  93.8 1.3 collective-permute-start
  95.1 0.1 pad_bitcast_fusion
  95.3 0.8 copy.22
  96.1 0.1 slice.45
  96.2 1.2 reshape.31
  97.4 19.7 %psum.35 = f32[64]{0:T(128)S(1)} all-reduce(f32[64]{0:T(128)S(1)} %multiply_reduce_fusion.1), channel_id=1, replica_groups=mesh['tm'=4,'coef'=8] {'coef'}, use_global_device_ids=true, to_apply=%region_1.0 | all-reduce | flops 64 | bytes 512 | tf_op jit(solution)/shard_map/psum | solution.py:80
  117.1 0.0 collective-permute-done
  117.1 0.0 copy-done.5
  117.2 0.1 pad_maximum_fusion
  117.3 1.2 multiply_reduce_fusion.2
  118.6 5.7 %psum.37 = f32[64]{0:T(128)S(1)} all-reduce(f32[64]{0:T(128)S(1)} %get-tuple-element.9), channel_id=1, replica_groups=mesh['tm'=4,'coef'=8] {'tm'}, use_global_device_ids=true, to_apply=%region_4.0 | all-reduce | flops 64 | bytes 512 | tf_op jit(solution)/shard_map/psum | solution.py:83
  124.3 0.1 multiply_subtract_fusion
  124.3 0.0 copy-start.4
  124.4 0.8 fusion
  125.2 0.0 copy-done.4
  125.3 1.3 collective-permute-start.1
  126.6 1.8 collective-permute-done.1
  128.4 10.1 %convolution_bitcast_fusion = f32[5120,64]{0,1:T(8,128)} fusion(f32[512,5120]{1,0:T(8,128)} %param.6, f32[768,64]{0,1:T(8,128)S(1)} %bitcast.26, f32[255,64]{0,1:T(8,128)S(1)} %collective-permute-done.1), kind=kOutput, calls=%fused_computation | convolution fusion | flops 2013298688 | bytes 11993088 | tf_op jit(solution)/shard_map/dot_general | solution.py:65
  138.5 0.0 all-reduce.11.cloned.1.call-update
  138.6 37.9 %all-reduce.11.cloned.1.call-done = f32[5120,64]{0,1:T(8,128)} async-done(((f32[5120,64]{0,1:T(8,128)}), f32[5120,64]{0,1:T(8,128)}) %all-reduce.11.cloned.1.call-update) | async-done | bytes 1310736 | tf_op jit(solution)/shard_map/psum | solution.py:92
  176.4 1.6 multiply_reduce_fusion
  178.0 21.4 %psum.39 = f32[64]{0:T(128)S(1)} all-reduce(f32[64]{0:T(128)S(1)} %multiply_reduce_fusion), channel_id=1, replica_groups=mesh['tm'=4,'coef'=8] {'coef'}, use_global_device_ids=true, to_apply=%region_7.0 | all-reduce | flops 64 | bytes 512 | tf_op jit(solution)/shard_map/psum | solution.py:93
  199.4 3.1 %multiply_add_fusion = (f32[5120,64]{0,1:T(8,128)}, f32[5120,64]{0,1:T(8,128)}) fusion(f32[5120,64]{0,1:T(8,128)S(1)} %copy-done.1, f32[5120,64]{0,1:T(8,128)S(1)} %copy-done, f32[64]{0:T(128)S(1)} %div.7, f32[5120,64]{0,1:T(8,128)} %param.8, f32[64]{0:T(128)S(1)} %div.6), kind=kLoop, calls=%fused_computation.1 | loop fusion | flops 1310720 | bytes 6554112 | tf_op jit(solution)/shard_map/add | solution.py:94
  (18 shorter events, 0.1 us)
Async XLA Ops:
  7.2 13.3 %copy-start.3 = (f32[512,256]{1,0:T(8,128)S(1)}, f32[512,256]{1,0:T(8,128)}, u32[]{:S(2)}) copy-start(f32[512,256]{1,0:T(8,128)} %param.7) | copy-start | bytes 1572868
  7.2 85.8 %all-reduce.9.cloned.1.call-start = ((), (), s32[]{:S(2)}) async-start(), calls=%async_computation | async-start | bytes 262144 | tf_op jit(solution)/shard_map/psum | solution.py:80
  7.2 14.0 %copy-start.2 = (f32[5120,64]{0,1:T(8,128)S(1)}, f32[5120,64]{0,1:T(8,128)}, u32[]{:S(2)}) copy-start(f32[5120,64]{0,1:T(8,128)} %param.10) | copy-start | bytes 3932164
  20.4 156.0 %all-reduce.11.cloned.1.call-start = ((), (), s32[]{:S(2)}) async-start(), calls=%async_computation.1 | async-start | bytes 2621440 | tf_op jit(solution)/shard_map/psum | solution.py:92
  93.8 23.3 %collective-permute-start = (f32[255,64]{0,1:T(8,128)S(1)}, f32[255,64]{0,1:T(8,128)S(1)}, u32[]{:S(2)}, u32[]{:S(2)}) collective-permute-start(f32[255,64]{0,1:T(8,128)S(1)} %slice.46), channel_id=1, source_target_pairs={{0,8},{8,16},{16,24},{1,9},{9,17},{17,25},{2,10},{10,18},{18,26},{... | collective-permute-start | bytes 195848 | tf_op jit(solution)/shard_map/ppermute | solution.py:10
  96.2 21.0 %copy-start.5 = (f32[512,64]{0,1:T(8,128)S(1)}, f32[512,64]{0,1:T(8,128)}, u32[]{:S(2)}) copy-start(f32[512,64]{0,1:T(8,128)} %all-reduce.9.cloned.1.call-done) | copy-start | bytes 393220
  117.1 7.1 %copy-start.6 = (f32[512,64]{0,1:T(8,128)S(1)}, f32[512,64]{0,1:T(8,128)}, u32[]{:S(2)}) copy-start(f32[512,64]{0,1:T(8,128)} %param.11) | copy-start | bytes 393220
  124.3 0.9 copy-start.4
  125.3 3.1 %collective-permute-start.1 = (f32[255,64]{0,1:T(8,128)S(1)}, f32[255,64]{0,1:T(8,128)S(1)}, u32[]{:S(2)}, u32[]{:S(2)}) collective-permute-start(f32[255,64]{0,1:T(8,128)S(1)} %slice.50), channel_id=1, source_target_pairs={{8,0},{16,8},{24,16},{9,1},{17,9},{25,17},{10,2},{18,10},{26,18},{... | collective-permute-start | bytes 195848 | tf_op jit(solution)/shard_map/ppermute | solution.py:10
  138.5 60.9 %copy-start = (f32[5120,64]{0,1:T(8,128)S(1)}, f32[5120,64]{0,1:T(8,128)}, u32[]{:S(2)}) copy-start(f32[5120,64]{0,1:T(8,128)} %param.9) | copy-start | bytes 3932164
  176.4 23.0 %copy-start.1 = (f32[5120,64]{0,1:T(8,128)S(1)}, f32[5120,64]{0,1:T(8,128)}, u32[]{:S(2)}) copy-start(f32[5120,64]{0,1:T(8,128)} %all-reduce.11.cloned.1.call-done) | copy-start | bytes 3932164
Sparse Core Ops, SparseCore 0:
  20.5 72.3 all-reduce.8
  138.7 37.7 all-reduce.10
where the time goes:
time: 210 us; the launch traced here: 209 us
  waiting for transfers between devices  111 us (53%)
  blocking collectives  46.7 us (22%)
  matrix products  25.3 us (12%)
  between operations  14.2 us (7%)
  other arithmetic  5.15 us (2%)
  local copies, waits for them, and re-layouts  3.98 us (2%)
  starting transfers between devices  2.66 us (1%)
    psum x1, waiting for transfers between devices, per_device(): totals, old_norm = lax.psum((partial_value, old_part), 'coef')  71.5 us
    psum x1, waiting for transfers between devices, per_device(): gradient = lax.psum(grad_part, 'tm')  37.9 us
    psum x1, blocking collectives, per_device(): new_norm = lax.psum(jnp.sum(gradient * gradient, axis=0), 'coef')  21.4 us
    psum x1, blocking collectives, per_device(): totals, old_norm = lax.psum((partial_value, old_part), 'coef')  19.7 us
    dot_general x1, matrix products, product(): jnp.dot(left, right, precision=lax.Precision.HIGHEST, preferred_element_t...  13.2 us
    dot_general x1, matrix products, product_left_t(): lax.dot_general(left, right, (((0,), (0,)), ((), ())), precision=lax.Prec...  10.1 us
    psum x1, blocking collectives, per_device(): energy = lax.psum(jnp.sum(predicted * predicted, axis=0), 'tm')  5.66 us
  transfers between devices with their start and end apart: 4, of which 3 were waited for; matrix products, arithmetic and copies ran while one was open for 2% of the time, Pallas kernels for 0%

commit v1 on v0

v1 whole, which is shorter than its diff:
```python
import functools

import jax
import jax.numpy as jnp
from jax import lax
from jax.experimental import pallas as pl
from jax.experimental.pallas import tpu as pltpu
from jax.sharding import PartitionSpec as P

F32 = jnp.float32
BF16 = jnp.bfloat16
LANES = 128


def chunk_width(columns):
    for width in (512, 384, 256, 128):
        if columns % (2 * width) == 0:
            return width
    return columns // 2


def split(x):
    hi = x.astype(BF16)
    return hi, (x - hi.astype(F32)).astype(BF16)


def dot_nt(a, b):
    return lax.dot_general(a, b, (((1,), (1,)), ((), ())), preferred_element_type=F32)


def dot_nn(a, b):
    return jnp.dot(a, b, preferred_element_type=F32)


def lane_fold(x):
    total = x[:, :LANES]
    for at in range(LANES, x.shape[1], LANES):
        total = total + x[:, at : at + LANES]
    return total


def total_over_lanes(x):
    return jnp.broadcast_to(jnp.sum(x, axis=1, keepdims=True), x.shape)


def widen(x, columns):
    return jnp.concatenate([x] * (columns // LANES), axis=1)


def kernel(
    ntm, ncoef,
    design, whitening, sol, direction, gprev, resid,
    nsol_out, nres_out, ndir_out,
    df, dhi, dlo, dv, gp, sv, rv, wv, acc, band_hi, band_lo,
    rs_send, rs_recv, halo_send, halo_recv, e_buf, carry_send, carry_recv,
    ag_buf, ag2_buf, white, nres, nsol, psend, precv, xbuf, gbuf, nd, n_buf,
    sem_d, sem_v, sem_in, sem_out, sem_nd,
    rs_s, rs_r, halo_s, halo_r, e_s, e_r, carry_s, carry_r,
    ag_s, ag_r, ag2_s, ag2_r, pair_s, pair_r, x_s, x_r, fin_s, fin_r, n_s, n_r,
):
    nch, count, width = df.shape
    half = nch // 2
    nchip = ntm // 2
    right_sides = dv.shape[1]
    rpc = right_sides // ncoef
    bw = whitening.shape[1]
    nblocks = count // bw
    tm = lax.axis_index("tm")
    coef = lax.axis_index("coef")
    core = lax.rem(tm, 2)
    chip = tm // 2
    partner = chip * 2 + (1 - core)
    MESH = pl.DeviceIdType.MESH

    def remote(src, dst, send, recv, to):
        copy = pltpu.make_async_remote_copy(
            src_ref=src, dst_ref=dst, send_sem=send, recv_sem=recv,
            device_id=to, device_id_type=MESH,
        )
        return copy

    wh_copy = pltpu.make_async_copy(whitening, wv, sem_in.at[0])
    wh_copy.start()

    def cols(i):
        return pl.ds(pl.multiple_of(i * width, width), width)

    def d_copy(i):
        return pltpu.make_async_copy(design.at[:, cols(i)], df.at[i], sem_d.at[i])

    def v_copy(i):
        return pltpu.make_async_copy(direction.at[:, cols(i)], dv.at[i], sem_v.at[i])

    for i in range(nch):
        v_copy(i).start()
        d_copy(i).start()
    gp_copy = pltpu.make_async_copy(gprev, gp, sem_in.at[1])
    gp_copy.start()
    res_copy = pltpu.make_async_copy(resid, rv, sem_in.at[2])
    res_copy.start()
    sol_copy = pltpu.make_async_copy(sol, sv, sem_in.at[3])
    sol_copy.start()

    barrier = pltpu.get_barrier_semaphore()
    greeted = 0
    for d in range(ncoef):
        other = lax.rem(coef + d, ncoef)
        if d:
            pl.semaphore_signal(barrier, inc=1, device_id=(tm, other), device_id_type=MESH)
            greeted += 1
            pl.semaphore_signal(barrier, inc=1, device_id=(partner, other), device_id_type=MESH)
            greeted += 1
    for d in range(1, ntm):
        pl.semaphore_signal(
            barrier, inc=1, device_id=(lax.rem(tm + d, ntm), coef), device_id_type=MESH
        )
        greeted += 1

    wh_copy.wait()
    mirror = (
        lax.broadcasted_iota(jnp.int32, (bw, bw), 0)
        + lax.broadcasted_iota(jnp.int32, (bw, bw), 1)
        == bw - 1
    ).astype(F32)
    for b in range(nblocks):
        taps = jnp.dot(
            wv[b * bw : (b + 1) * bw, :], mirror,
            precision=lax.Precision.HIGHEST, preferred_element_type=F32,
        )
        padded = jnp.concatenate([taps, jnp.zeros((bw, bw), F32)], axis=1)
        band = pltpu.roll(padded, 1, 1, stride=1, stride_axis=0)
        hi, lo = split(band)
        band_hi[b] = hi
        band_lo[b] = lo

    acc[...] = jnp.zeros_like(acc)

    def forward(i, carry):
        d_copy(i).wait()
        v_copy(i).wait()
        hi, lo = split(df[i])
        dhi[i] = hi
        dlo[i] = lo
        vhi = dv[i].astype(BF16).astype(F32)
        both = jnp.concatenate([vhi, dv[i] - vhi], axis=0).astype(BF16)
        acc[...] += dot_nt(hi, both) + dot_nt(lo, both)
        return carry

    lax.fori_loop(0, nch, forward, 0)
    turned = acc[...].T
    partial = turned[:right_sides] + turned[right_sides:]
    gp_copy.wait()
    old_lanes = jnp.zeros((right_sides, LANES), F32)
    for i in range(nch):
        g = gp[:, i * width : (i + 1) * width]
        old_lanes = old_lanes + lane_fold(g * g)
    for j in range(ncoef):
        rs_send[j, :, :count] = partial[j * rpc : (j + 1) * rpc]
        rs_send[j, :, count:] = old_lanes[j * rpc : (j + 1) * rpc]

    pl.semaphore_wait(barrier, greeted)
    sends = []

    def start(copy):
        copy.start()
        sends.append(copy)

    peers = [lax.rem(coef + d, ncoef) for d in range(1, ncoef)]
    for j in peers:
        start(remote(rs_send.at[j], rs_recv.at[coef], rs_s.at[j], rs_r.at[coef], (tm, j)))
    rs_recv[coef] = rs_send[coef]

    res_copy.wait()
    for j in range(ncoef):
        ag2_buf[j, :, :count] = rv[j * rpc : (j + 1) * rpc, :]
    my_res = ag2_buf[coef][:, :count]

    def back(values):
        hi, lo = split(values)
        pieces = []
        for b in range(nblocks):
            h = hi[:, b * bw : (b + 1) * bw]
            l = lo[:, b * bw : (b + 1) * bw]
            pieces.append(
                dot_nn(h, band_hi[b]) + dot_nn(l, band_hi[b]) + dot_nn(h, band_lo[b])
            )
        out = [pieces[0][:, :bw]]
        for b in range(nblocks):
            tail = pieces[b][:, bw:]
            out.append(tail + pieces[b + 1][:, :bw] if b + 1 < nblocks else tail)
        return out[0], jnp.concatenate(out[1:], axis=1)

    res_out, res_in = back(my_res)

    for j in peers:
        remote(rs_send.at[j], rs_recv.at[j], rs_s.at[j], rs_r.at[j], (tm, j)).wait_recv()
    mine = rs_recv[0]
    for j in range(1, ncoef):
        mine = mine + rs_recv[j]
    total = mine[:, :count]
    old_norm = total_over_lanes(mine[:, count:])
    halo_send[...] = total[:, count - bw :]
    after = lax.rem(tm + 1, ntm)
    before = lax.rem(tm + ntm - 1, ntm)
    halo = remote(halo_send, halo_recv, halo_s, halo_r, (after, coef))
    start(halo)

    def forth(window, b):
        hi, lo = split(window)
        return dot_nt(hi, band_hi[b]) + dot_nt(lo, band_hi[b]) + dot_nt(hi, band_lo[b])

    later = [forth(total[:, (b - 1) * bw : (b + 1) * bw], b) for b in range(1, nblocks)]
    halo.wait_recv()
    edge = jnp.where(tm == 0, jnp.zeros_like(halo_recv[...]), halo_recv[...])
    first = forth(jnp.concatenate([edge, total[:, :bw]], axis=1), 0)
    predicted = jnp.concatenate([first] + later, axis=1)
    e_buf[tm] = lane_fold(predicted * predicted)
    for d in range(1, ntm):
        other = lax.rem(tm + d, ntm)
        start(remote(e_buf.at[tm], e_buf.at[tm], e_s.at[other], e_r.at[tm], (other, coef)))
    pred_out, pred_in = back(predicted)
    carry_send[:, :bw] = res_out
    carry_send[:, bw:] = pred_out
    carry = remote(carry_send, carry_recv, carry_s, carry_r, (before, coef))
    start(carry)
    for d in range(1, ntm):
        other = lax.rem(tm + d, ntm)
        remote(e_buf.at[other], e_buf.at[other], e_s.at[other], e_r.at[other], (other, coef)).wait_recv()
    energy = e_buf[0]
    for t in range(1, ntm):
        energy = energy + e_buf[t]
    step = old_norm / total_over_lanes(energy)
    carry.wait_recv()
    last = tm == ntm - 1
    carried = jnp.where(last, jnp.zeros_like(carry_recv[...]), carry_recv[...])

    def with_carried(inner, extra):
        tail = inner[:, count - bw :] + extra
        if count == bw:
            return tail
        return jnp.concatenate([inner[:, : count - bw], tail], axis=1)

    step_wide = widen(step, count)
    ag_buf[coef] = with_carried(res_in, carried[:, :bw]) - step_wide * with_carried(
        pred_in, carried[:, bw:]
    )
    for j in peers:
        start(remote(ag_buf.at[coef], ag_buf.at[coef], ag_s.at[j], ag_r.at[coef], (tm, j)))
    ag2_buf[coef, :, :count] = my_res - step_wide * predicted
    ag2_buf[coef, :, count : count + LANES] = step
    ag2_buf[coef, :, count + LANES :] = old_norm
    for j in peers:
        remote(ag_buf.at[j], ag_buf.at[j], ag_s.at[j], ag_r.at[j], (tm, j)).wait_recv()
    for j in range(ncoef):
        white[j * rpc : (j + 1) * rpc, :] = ag_buf[j]
    whi = white[...].astype(BF16)
    whi32 = whi.astype(F32)
    wboth = jnp.concatenate([whi32, white[...] - whi32], axis=0).astype(BF16)

    def grad_chunk(i):
        a = dot_nn(wboth, dhi[i])
        return a[:right_sides] + a[right_sides:] + dot_nn(whi, dlo[i])

    def to_chips(k):
        remote(psend.at[k], precv.at[k], pair_s.at[k], pair_r.at[k], (partner, coef)).wait_recv()
        xbuf[chip, k] = xbuf[chip, k] + precv[k]
        for q in range(1, nchip):
            other = lax.rem(chip + q, nchip)
            start(
                remote(
                    xbuf.at[chip, k], xbuf.at[chip, k], x_s.at[other, k], x_r.at[chip, k],
                    (other * 2 + core, coef),
                )
            )

    for k in range(half):
        psend[k] = grad_chunk((1 - core) * half + k)
        start(remote(psend.at[k], precv.at[k], pair_s.at[k], pair_r.at[k], (partner, coef)))
        xbuf[chip, k] = grad_chunk(core * half + k)
        to_chips(k)
        if k == 0:
            for j in peers:
                start(
                    remote(ag2_buf.at[coef], ag2_buf.at[coef], ag2_s.at[j], ag2_r.at[coef], (tm, j))
                )

    for j in peers:
        remote(ag2_buf.at[j], ag2_buf.at[j], ag2_s.at[j], ag2_r.at[j], (tm, j)).wait_recv()
    tails = []
    for j in range(ncoef):
        nres[j * rpc : (j + 1) * rpc, :] = ag2_buf[j][:, :count]
        tails.append(ag2_buf[j][:, count:])
    tail = jnp.concatenate(tails, axis=0)
    step_all = widen(tail[:, :LANES], width)
    old_all = tail[:, LANES:]
    nres_copy = pltpu.make_async_copy(nres, nres_out, sem_out.at[0])
    nres_copy.start()
    sol_copy.wait()
    for i in range(nch):
        at = slice(i * width, (i + 1) * width)
        nsol[:, at] = sv[:, at] + step_all * dv[i]
    nsol_copy = pltpu.make_async_copy(nsol, nsol_out, sem_out.at[1])
    nsol_copy.start()

    squares = jnp.zeros((right_sides, LANES), F32)
    for k in range(half):
        for q in range(1, nchip):
            other = lax.rem(chip + q, nchip)
            remote(
                xbuf.at[other, k], xbuf.at[other, k], x_s.at[other, k], x_r.at[other, k],
                (other * 2 + core, coef),
            ).wait_recv()
        g = xbuf[0, k]
        for t in range(1, nchip):
            g = g + xbuf[t, k]
        at = core * half + k
        gbuf[at] = g
        start(remote(gbuf.at[at], gbuf.at[at], fin_s.at[k], fin_r.at[k], (partner, coef)))
        squares = squares + lane_fold(g * g)

    slot = coef * 2 + core
    row = jnp.sum(squares.T, axis=0, keepdims=True)
    n_buf[slot] = jnp.concatenate([row, jnp.zeros((1, LANES - right_sides), F32)], axis=1)
    others = [(tm, j, j * 2 + core) for j in peers]
    others += [(partner, j, j * 2 + (1 - core)) for j in [coef] + peers]
    for t, j, s in others:
        start(remote(n_buf.at[slot], n_buf.at[slot], n_s.at[s], n_r.at[slot], (t, j)))
    for k in range(half):
        at = (1 - core) * half + k
        remote(gbuf.at[at], gbuf.at[at], fin_s.at[k], fin_r.at[k], (partner, coef)).wait_recv()
    for t, j, s in others:
        remote(n_buf.at[s], n_buf.at[s], n_s.at[s], n_r.at[s], (t, j)).wait_recv()
    row = n_buf[0]
    for s in range(1, 2 * ncoef):
        row = row + n_buf[s]
    new_all = jnp.broadcast_to(row, (LANES, LANES)).T[:right_sides]
    ratio = widen(new_all / old_all, width)
    outs = []
    for i in range(nch):
        nd[i] = gbuf[i] + ratio * dv[i]
        copy = pltpu.make_async_copy(
            nd.at[i], ndir_out.at[:, i * width : (i + 1) * width], sem_nd.at[i]
        )
        copy.start()
        outs.append(copy)
    for copy in sends:
        copy.wait_send()
    nres_copy.wait()
    nsol_copy.wait()
    for copy in outs:
        copy.wait()


def per_device(ntm, ncoef, design, whitening, solution, direction, gradient_prev, residual):
    count, columns = design.shape
    bw = whitening.shape[1]
    rs = direction.shape[1]
    rpc = rs // ncoef
    width = chunk_width(columns)
    nch = columns // width
    half = nch // 2
    nchip = ntm // 2
    nblocks = count // bw
    V = pltpu.VMEM
    D = pltpu.SemaphoreType.DMA
    any_spec = pl.BlockSpec(memory_space=pl.ANY)
    scratch = [
        V((nch, count, width), F32),
        V((nch, count, width), BF16),
        V((nch, count, width), BF16),
        V((nch, rs, width), F32),
        V((rs, columns), F32),
        V((rs, columns), F32),
        V((rs, count), F32),
        V((count, bw), F32),
        V((count, 2 * rs), F32),
        V((nblocks, bw, 2 * bw), BF16),
        V((nblocks, bw, 2 * bw), BF16),
        V((ncoef, rpc, count + LANES), F32),
        V((ncoef, rpc, count + LANES), F32),
        V((rpc, bw), F32),
        V((rpc, bw), F32),
        V((ntm, rpc, LANES), F32),
        V((rpc, 2 * bw), F32),
        V((rpc, 2 * bw), F32),
        V((ncoef, rpc, count), F32),
        V((ncoef, rpc, count + 2 * LANES), F32),
        V((rs, count), F32),
        V((rs, count), F32),
        V((rs, columns), F32),
        V((half, rs, width), F32),
        V((half, rs, width), F32),
        V((nchip, half, rs, width), F32),
        V((nch, rs, width), F32),
        V((nch, rs, width), F32),
        V((2 * ncoef, 1, LANES), F32),
        D((nch,)), D((nch,)), D((4,)), D((2,)), D((nch,)),
        D((ncoef,)), D((ncoef,)), D, D, D((ntm,)), D((ntm,)), D, D,
        D((ncoef,)), D((ncoef,)), D((ncoef,)), D((ncoef,)),
        D((half,)), D((half,)), D((nchip, half)), D((nchip, half)),
        D((half,)), D((half,)), D((2 * ncoef,)), D((2 * ncoef,)),
    ]
    outs = pl.pallas_call(
        functools.partial(kernel, ntm, ncoef),
        out_shape=(
            jax.ShapeDtypeStruct((rs, columns), F32),
            jax.ShapeDtypeStruct((rs, count), F32),
            jax.ShapeDtypeStruct((rs, columns), F32),
        ),
        in_specs=[any_spec] * 6,
        out_specs=(any_spec,) * 3,
        scratch_shapes=scratch,
        compiler_params=pltpu.CompilerParams(
            collective_id=0, has_side_effects=True, vmem_limit_bytes=56 * 2**20
        ),
        cost_estimate=pl.CostEstimate(
            flops=12 * count * columns * rs,
            bytes_accessed=4 * (count * columns + 5 * rs * columns),
            transcendentals=0,
        ),
    )(design, whitening, solution.T, direction.T, gradient_prev.T, residual.T)
    return tuple(o.T for o in outs)


def solution(mesh):
    ntm, ncoef = mesh.shape["tm"], mesh.shape["coef"]
    return jax.shard_map(
        functools.partial(per_device, ntm, ncoef),
        mesh=mesh,
        in_specs=(
            P("tm", "coef"),
            P("tm", None),
            P("coef", None),
            P("coef", None),
            P("coef", None),
            P("tm", None),
        ),
        out_specs=(P("coef", None), P("tm", None), P("coef", None)),
        check_vma=False,
    )
```

time: 210 us -> 55.7 us (0.27)
  waiting for transfers between devices: 111 us -> 0 us
  Pallas kernels: 0 us -> 50.6 us
  blocking collectives: 46.7 us -> 0 us
  matrix products: 25.3 us -> 0 us
  between operations: 14.2 us -> 0.66 us
  other arithmetic: 5.15 us -> 0 us
  starting transfers between devices: 2.66 us -> 0 us
    psum x2 -> x0, waiting for transfers between devices: 109 us -> none  [the longest x1 71.5 us: per_device(): totals, old_norm = lax.psum((partial_value, old_part), 'coef')]
    pallas_call x0 -> x1, Pallas kernels: none -> 50.6 us  [per_device(): pl.pallas_call(functools.partial(kernel, ntm, ncoef), out_shape=(jax.Shap...]
    psum x3 -> x0, blocking collectives: 46.7 us -> none  [the longest x1 21.4 us: per_device(): new_norm = lax.psum(jnp.sum(gradient * gradient, axis=0), 'coef')]
    dot_general x4 -> x0, matrix products: 25.3 us -> none  [the longest x1 13.2 us: product(): jnp.dot(left, right, precision=lax.Precision.HIGHEST, preferred_element_t...]
    unnamed x16 -> x7, local copies, waits for them, and re-layouts: 0.97 us -> 4.3 us
    add x1 -> x0, other arithmetic: 3.11 us -> none  [per_device(): new_direction = gradient + new_norm / old_norm * direction]
    ppermute x2 -> x0, starting transfers between devices: 2.58 us -> none  [shifted(): return lax.ppermute(array, axis, pairs)]
  transfers between devices with their start and end apart: 4 -> 0, of which waited for: 3 -> 0; matrix products, arithmetic and copies ran while one was open for 2% -> 0% of each run, Pallas kernels for 0% -> 0%
where the time goes in v1:
time: 55.7 us; the launch traced here: 55.6 us
  Pallas kernels  50.6 us (91%)
  local copies, waits for them, and re-layouts  4.3 us (8%)
  between operations  0.66 us (1%)
    pallas_call x1, Pallas kernels, per_device(): pl.pallas_call(functools.partial(kernel, ntm, ncoef), out_shape=(jax.Shap...  50.6 us
    unnamed x7, local copies, waits for them, and re-layouts  4.3 us

profile of v1, /device:TPU:0, one launch (start us, length us, event | category | flops | bytes accessed | tf_op | source)
XLA Modules:
  0.0 55.6 jit_solution(10213946357366095477)
XLA Ops:
  0.6 50.6 %shard_map.85 = (f32[64,5120]{1,0:T(8,128)}, f32[64,512]{1,0:T(8,128)}, f32[64,5120]{1,0:T(8,128)}) custom-call(f32[512,5120]{1,0:T(8,128)} %design.1, f32[512,256]{1,0:T(8,128)} %whitening.1, f32[64,5120]{1,0:T(8,128)} %bitcast.7, f32[64,5120]{1,0:T(8,128)} %bitcast.8, f32[64,5120]{1,0:T(8,128)} %bitcast.9, f32[64,512]{1,0:T(8,128)} %bitcast.12), custom_call_target="tpu_custom_call" | custom-call | flops 2013265920 | bytes 17039360 | tf_op jit(solution)/shard_map/pallas_call | solution.py:403
  51.2 0.0 copy-start.1
  51.2 0.0 copy-start
  51.3 2.6 %copy.12 = f32[5120,64]{0,1:T(8,128)} copy(f32[5120,64]{0,1:T(8,128)} %bitcast.11) | data formatting | bytes 2621440
  53.8 0.0 copy-done.1
  53.8 0.7 %copy.13 = f32[512,64]{0,1:T(8,128)} copy(f32[512,64]{0,1:T(8,128)S(1)} %bitcast.13) | data formatting | bytes 262144
  54.5 0.0 copy-done
  54.5 1.1 %copy.14 = f32[5120,64]{0,1:T(8,128)} copy(f32[5120,64]{0,1:T(8,128)S(1)} %bitcast.10) | data formatting | bytes 2621440
Async XLA Ops:
  51.2 2.6 %copy-start.1 = (f32[64,512]{1,0:T(8,128)S(1)}, f32[64,512]{1,0:T(8,128)}, u32[]{:S(2)}) copy-start(f32[64,512]{1,0:T(8,128)} %get-tuple-element.7) | copy-start | bytes 393220
  51.2 3.2 %copy-start = (f32[64,5120]{1,0:T(8,128)S(1)}, f32[64,5120]{1,0:T(8,128)}, u32[]{:S(2)}) copy-start(f32[64,5120]{1,0:T(8,128)} %get-tuple-element.8) | copy-start | bytes 3932164

commit v2 on v1

--- a/solution.py
+++ b/solution.py
@@ -49,12 +49,12 @@
 
 def kernel(
     ntm, ncoef,
-    design, whitening, sol, direction, gprev, resid,
-    nsol_out, nres_out, ndir_out,
-    df, dhi, dlo, dv, gp, sv, rv, wv, acc, band_hi, band_lo,
+    design, whitening, direction, gprev, resid,
+    nres, grad, scale,
+    df, dhi, dlo, dv, gp, rv, wv, acc, band_hi, band_lo,
     rs_send, rs_recv, halo_send, halo_recv, e_buf, carry_send, carry_recv,
-    ag_buf, ag2_buf, white, nres, nsol, psend, precv, xbuf, gbuf, nd, n_buf,
-    sem_d, sem_v, sem_in, sem_out, sem_nd,
+    ag_buf, ag2_buf, white, psend, precv, xbuf, gbuf, n_buf,
+    sem_d, sem_v, sem_in,
     rs_s, rs_r, halo_s, halo_r, e_s, e_r, carry_s, carry_r,
     ag_s, ag_r, ag2_s, ag2_r, pair_s, pair_r, x_s, x_r, fin_s, fin_r, n_s, n_r,
 ):
@@ -98,8 +98,6 @@
     gp_copy.start()
     res_copy = pltpu.make_async_copy(resid, rv, sem_in.at[2])
     res_copy.start()
-    sol_copy = pltpu.make_async_copy(sol, sv, sem_in.at[3])
-    sol_copy.start()
 
     barrier = pltpu.get_barrier_semaphore()
     greeted = 0
@@ -291,16 +289,8 @@
         nres[j * rpc : (j + 1) * rpc, :] = ag2_buf[j][:, :count]
         tails.append(ag2_buf[j][:, count:])
     tail = jnp.concatenate(tails, axis=0)
-    step_all = widen(tail[:, :LANES], width)
+    scale[0] = tail[:, :LANES]
     old_all = tail[:, LANES:]
-    nres_copy = pltpu.make_async_copy(nres, nres_out, sem_out.at[0])
-    nres_copy.start()
-    sol_copy.wait()
-    for i in range(nch):
-        at = slice(i * width, (i + 1) * width)
-        nsol[:, at] = sv[:, at] + step_all * dv[i]
-    nsol_copy = pltpu.make_async_copy(nsol, nsol_out, sem_out.at[1])
-    nsol_copy.start()
 
     squares = jnp.zeros((right_sides, LANES), F32)
     for k in range(half):
@@ -334,21 +324,11 @@
     for s in range(1, 2 * ncoef):
         row = row + n_buf[s]
     new_all = jnp.broadcast_to(row, (LANES, LANES)).T[:right_sides]
-    ratio = widen(new_all / old_all, width)
-    outs = []
+    scale[1] = new_all / old_all
     for i in range(nch):
-        nd[i] = gbuf[i] + ratio * dv[i]
-        copy = pltpu.make_async_copy(
-            nd.at[i], ndir_out.at[:, i * width : (i + 1) * width], sem_nd.at[i]
-        )
-        copy.start()
-        outs.append(copy)
+        grad[:, i * width : (i + 1) * width] = gbuf[i]
     for copy in sends:
         copy.wait_send()
-    nres_copy.wait()
-    nsol_copy.wait()
-    for copy in outs:
-        copy.wait()
 
 
 def per_device(ntm, ncoef, design, whitening, solution, direction, gradient_prev, residual):
@@ -363,13 +343,11 @@
     nblocks = count // bw
     V = pltpu.VMEM
     D = pltpu.SemaphoreType.DMA
-    any_spec = pl.BlockSpec(memory_space=pl.ANY)
     scratch = [
         V((nch, count, width), F32),
         V((nch, count, width), BF16),
         V((nch, count, width), BF16),
         V((nch, rs, width), F32),
-        V((rs, columns), F32),
         V((rs, columns), F32),
         V((rs, count), F32),
         V((count, bw), F32),
@@ -386,40 +364,41 @@
         V((ncoef, rpc, count), F32),
         V((ncoef, rpc, count + 2 * LANES), F32),
         V((rs, count), F32),
-        V((rs, count), F32),
-        V((rs, columns), F32),
         V((half, rs, width), F32),
         V((half, rs, width), F32),
         V((nchip, half, rs, width), F32),
         V((nch, rs, width), F32),
-        V((nch, rs, width), F32),
         V((2 * ncoef, 1, LANES), F32),
-        D((nch,)), D((nch,)), D((4,)), D((2,)), D((nch,)),
+        D((nch,)), D((nch,)), D((3,)),
         D((ncoef,)), D((ncoef,)), D, D, D((ntm,)), D((ntm,)), D, D,
         D((ncoef,)), D((ncoef,)), D((ncoef,)), D((ncoef,)),
         D((half,)), D((half,)), D((nchip, half)), D((nchip, half)),
         D((half,)), D((half,)), D((2 * ncoef,)), D((2 * ncoef,)),
     ]
-    outs = pl.pallas_call(
+    new_residual, gradient, scale = pl.pallas_call(
         functools.partial(kernel, ntm, ncoef),
         out_shape=(
-            jax.ShapeDtypeStruct((rs, columns), F32),
             jax.ShapeDtypeStruct((rs, count), F32),
             jax.ShapeDtypeStruct((rs, columns), F32),
+            jax.ShapeDtypeStruct((2, rs, LANES), F32),
         ),
-        in_specs=[any_spec] * 6,
-        out_specs=(any_spec,) * 3,
+        in_specs=[pl.BlockSpec(memory_space=pltpu.HBM)] * 5,
+        out_specs=(pl.BlockSpec(memory_space=pltpu.VMEM),) * 3,
         scratch_shapes=scratch,
         compiler_params=pltpu.CompilerParams(
-            collective_id=0, has_side_effects=True, vmem_limit_bytes=56 * 2**20
+            collective_id=0, has_side_effects=True, vmem_limit_bytes=54 * 2**20
         ),
         cost_estimate=pl.CostEstimate(
             flops=12 * count * columns * rs,
             bytes_accessed=4 * (count * columns + 5 * rs * columns),
             transcendentals=0,
         ),
-    )(design, whitening, solution.T, direction.T, gradient_prev.T, residual.T)
-    return tuple(o.T for o in outs)
+    )(design, whitening, direction.T, gradient_prev.T, residual.T)
+    step = scale[0, :, 0]
+    ratio = scale[1, :, 0]
+    new_solution = solution + step * direction
+    new_direction = gradient.T + ratio * direction
+    return new_solution, new_residual.T, new_direction
 
 
 def solution(mesh):

time: 55.7 us -> 56.8 us (1.020)
  other arithmetic: 0 us -> 3.19 us
  local copies, waits for them, and re-layouts: 4.3 us -> 1.55 us
  Pallas kernels: 50.6 us -> 51.2 us
    unnamed x7, local copies, waits for them, and re-layouts: 4.3 us -> 0.67 us
    add x0 -> x1, other arithmetic: none -> 3.19 us  [per_device(): new_direction = gradient.T + ratio * direction]
    slice x0 -> x1, local copies, waits for them, and re-layouts: none -> 0.88 us  [per_device(): ratio = scale[1, :, 0]]
    pallas_call x1, Pallas kernels: 50.6 us -> 51.2 us  [per_device(): pl.pallas_call(functools.partial(kernel, ntm, ncoef), out_shape=(jax.Shap...]
where the time goes in v2:
time: 56.8 us; the launch traced here: 56.6 us
  Pallas kernels  51.2 us (90%)
  other arithmetic  3.19 us (6%)
  local copies, waits for them, and re-layouts  1.55 us (3%)
  between operations  0.68 us (1%)
    pallas_call x1, Pallas kernels, per_device(): pl.pallas_call(functools.partial(kernel, ntm, ncoef), out_shape=(jax.Shap...  51.2 us
    add x1, other arithmetic, per_device(): new_direction = gradient.T + ratio * direction  3.19 us

profile of v2, /device:TPU:0, one launch (start us, length us, event | category | flops | bytes accessed | tf_op | source)
XLA Modules:
  0.0 56.6 jit_solution(3900140331137028137)
XLA Ops:
  0.6 0.0 copy-start
  0.6 0.0 copy-start.1
  0.7 51.2 %shard_map.85 = (f32[64,512]{1,0:T(8,128)}, f32[64,5120]{1,0:T(8,128)}, f32[2,64,128]{2,1,0:T(8,128)}) custom-call(f32[512,5120]{1,0:T(8,128)} %design.1, f32[512,256]{1,0:T(8,128)} %whitening.1, f32[64,5120]{1,0:T(8,128)} %bitcast.6, f32[64,5120]{1,0:T(8,128)} %bitcast.7, f32[64,512]{1,0:T(8,128)} %bitcast.8), custom_call_target="tpu_custom_call" | custom-call | flops 2013265920 | bytes 17039360 | tf_op jit(solution)/shard_map/pallas_call | solution.py:378
  51.9 0.9 %slice_reduce_fusion = (f32[64]{0:T(128)S(1)}, f32[64]{0:T(128)S(1)}) fusion(f32[2,64,128]{2,1,0:T(8,128)} %get-tuple-element.6), kind=kLoop, calls=%fused_computation.2 | loop fusion | bytes 1024 | tf_op jit(solution)/shard_map/slice | solution.py:398
  52.7 0.0 copy-done
  52.7 0.0 copy-done.1
  52.8 0.0 copy-start.2
  52.8 3.2 %bitcast_add_fusion = (f32[5120,64]{0,1:T(8,128)}, f32[5120,64]{0,1:T(8,128)}) fusion(f32[64,5120]{1,0:T(8,128)} %get-tuple-element.8, f32[5120,64]{0,1:T(8,128)S(1)} %copy-done, f32[64]{0:T(128)S(1)} %get-tuple-element.9, f32[5120,64]{0,1:T(8,128)S(1)} %copy-done.1, f32[64]{0:T(128)S(1)} %get-tuple-element.10), kind=kLoop, calls=%fused_computation | loop fusion | flops 1310720 | bytes 6554112 | tf_op jit(solution)/shard_map/add | solution.py:400
  56.0 0.0 copy-done.2
  56.0 0.7 %copy.10 = f32[512,64]{0,1:T(8,128)} copy(f32[512,64]{0,1:T(8,128)S(1)} %bitcast.9) | data formatting | bytes 262144
Async XLA Ops:
  0.6 52.1 %copy-start = (f32[5120,64]{0,1:T(8,128)S(1)}, f32[5120,64]{0,1:T(8,128)}, u32[]{:S(2)}) copy-start(f32[5120,64]{0,1:T(8,128)} %param.9) | copy-start | bytes 3932164
  0.6 52.1 %copy-start.1 = (f32[5120,64]{0,1:T(8,128)S(1)}, f32[5120,64]{0,1:T(8,128)}, u32[]{:S(2)}) copy-start(f32[5120,64]{0,1:T(8,128)} %param.8) | copy-start | bytes 3932164
  52.8 3.2 %copy-start.2 = (f32[64,512]{1,0:T(8,128)S(1)}, f32[64,512]{1,0:T(8,128)}, u32[]{:S(2)}) copy-start(f32[64,512]{1,0:T(8,128)} %get-tuple-element.7) | copy-start | bytes 393220

commit v3 on v1

--- a/solution.py
+++ b/solution.py
@@ -50,11 +50,11 @@
 def kernel(
     ntm, ncoef,
     design, whitening, sol, direction, gprev, resid,
-    nsol_out, nres_out, ndir_out,
+    nsol, nres, ndir,
     df, dhi, dlo, dv, gp, sv, rv, wv, acc, band_hi, band_lo,
     rs_send, rs_recv, halo_send, halo_recv, e_buf, carry_send, carry_recv,
-    ag_buf, ag2_buf, white, nres, nsol, psend, precv, xbuf, gbuf, nd, n_buf,
-    sem_d, sem_v, sem_in, sem_out, sem_nd,
+    ag_buf, ag2_buf, white, psend, precv, xbuf, gbuf, n_buf,
+    sem_d, sem_v, sem_in,
     rs_s, rs_r, halo_s, halo_r, e_s, e_r, carry_s, carry_r,
     ag_s, ag_r, ag2_s, ag2_r, pair_s, pair_r, x_s, x_r, fin_s, fin_r, n_s, n_r,
 ):
@@ -293,14 +293,10 @@
     tail = jnp.concatenate(tails, axis=0)
     step_all = widen(tail[:, :LANES], width)
     old_all = tail[:, LANES:]
-    nres_copy = pltpu.make_async_copy(nres, nres_out, sem_out.at[0])
-    nres_copy.start()
     sol_copy.wait()
     for i in range(nch):
         at = slice(i * width, (i + 1) * width)
         nsol[:, at] = sv[:, at] + step_all * dv[i]
-    nsol_copy = pltpu.make_async_copy(nsol, nsol_out, sem_out.at[1])
-    nsol_copy.start()
 
     squares = jnp.zeros((right_sides, LANES), F32)
     for k in range(half):
@@ -335,20 +331,10 @@
         row = row + n_buf[s]
     new_all = jnp.broadcast_to(row, (LANES, LANES)).T[:right_sides]
     ratio = widen(new_all / old_all, width)
-    outs = []
     for i in range(nch):
-        nd[i] = gbuf[i] + ratio * dv[i]
-        copy = pltpu.make_async_copy(
-            nd.at[i], ndir_out.at[:, i * width : (i + 1) * width], sem_nd.at[i]
-        )
-        copy.start()
-        outs.append(copy)
+        ndir[:, i * width : (i + 1) * width] = gbuf[i] + ratio * dv[i]
     for copy in sends:
         copy.wait_send()
-    nres_copy.wait()
-    nsol_copy.wait()
-    for copy in outs:
-        copy.wait()
 
 
 def per_device(ntm, ncoef, design, whitening, solution, direction, gradient_prev, residual):
@@ -386,15 +372,12 @@
         V((ncoef, rpc, count), F32),
         V((ncoef, rpc, count + 2 * LANES), F32),
         V((rs, count), F32),
-        V((rs, count), F32),
-        V((rs, columns), F32),
         V((half, rs, width), F32),
         V((half, rs, width), F32),
         V((nchip, half, rs, width), F32),
         V((nch, rs, width), F32),
-        V((nch, rs, width), F32),
         V((2 * ncoef, 1, LANES), F32),
-        D((nch,)), D((nch,)), D((4,)), D((2,)), D((nch,)),
+        D((nch,)), D((nch,)), D((4,)),
         D((ncoef,)), D((ncoef,)), D, D, D((ntm,)), D((ntm,)), D, D,
         D((ncoef,)), D((ncoef,)), D((ncoef,)), D((ncoef,)),
         D((half,)), D((half,)), D((nchip, half)), D((nchip, half)),
@@ -408,10 +391,10 @@
             jax.ShapeDtypeStruct((rs, columns), F32),
         ),
         in_specs=[any_spec] * 6,
-        out_specs=(any_spec,) * 3,
+        out_specs=(pl.BlockSpec(memory_space=pltpu.VMEM),) * 3,
         scratch_shapes=scratch,
         compiler_params=pltpu.CompilerParams(
-            collective_id=0, has_side_effects=True, vmem_limit_bytes=56 * 2**20
+            collective_id=0, has_side_effects=True, vmem_limit_bytes=51 * 2**20
         ),
         cost_estimate=pl.CostEstimate(
             flops=12 * count * columns * rs,

time: 55.7 us -> 53.7 us (0.964)
  Pallas kernels: 50.6 us -> 48.1 us
    pallas_call x1, Pallas kernels: 50.6 us -> 48.1 us  [per_device(): pl.pallas_call(functools.partial(kernel, ntm, ncoef), out_shape=(jax.Shap...]
    unnamed x7 -> x9, local copies, waits for them, and re-layouts: 4.3 us -> 4.78 us
where the time goes in v3:
time: 53.7 us; the launch traced here: 53.5 us
  Pallas kernels  48.1 us (90%)
  local copies, waits for them, and re-layouts  4.78 us (9%)
  between operations  0.66 us (1%)
    pallas_call x1, Pallas kernels, per_device(): pl.pallas_call(functools.partial(kernel, ntm, ncoef), out_shape=(jax.Shap...  48.1 us
    unnamed x9, local copies, waits for them, and re-layouts  4.78 us

profile of v3, /device:TPU:0, one launch (start us, length us, event | category | flops | bytes accessed | tf_op | source)
XLA Modules:
  0.0 53.5 jit_solution(18430713635357542631)
XLA Ops:
  0.6 0.0 copy-start
  0.6 1.0 %copy-done = f32[512,256]{1,0:T(8,128)S(1)} copy-done((f32[512,256]{1,0:T(8,128)S(1)}, f32[512,256]{1,0:T(8,128)}, u32[]{:S(2)}) %copy-start) | copy-done | bytes 524312
  1.7 0.0 copy-start.1
  1.7 0.9 %copy-done.1 = f32[512,64]{0,1:T(8,128)S(1)} copy-done((f32[512,64]{0,1:T(8,128)S(1)}, f32[512,64]{0,1:T(8,128)}, u32[]{:S(2)}) %copy-start.1) | copy-done | bytes 131096
  2.6 48.1 %shard_map.85 = (f32[64,5120]{1,0:T(8,128)S(1)}, f32[64,512]{1,0:T(8,128)S(1)}, f32[64,5120]{1,0:T(8,128)}) custom-call(f32[512,5120]{1,0:T(8,128)} %design.1, f32[512,256]{1,0:T(8,128)S(1)} %copy-done, f32[64,5120]{1,0:T(8,128)} %bitcast.10, f32[64,5120]{1,0:T(8,128)} %bitcast.11, f32[64,5120]{1,0:T(8,128)} %bitcast.12, f32[64,512]{1,0:T(8,128)S(1)} %bitcast.8), custom_call_target="tpu_custom_call" | custom-call | flops 2013265920 | bytes 17039360 | tf_op jit(solution)/shard_map/pallas_call | solution.py:386
  50.6 0.0 copy-start.2
  50.7 1.1 %copy.12 = f32[5120,64]{0,1:T(8,128)} copy(f32[5120,64]{0,1:T(8,128)S(1)} %bitcast.7) | data formatting | bytes 2621440
  51.7 0.7 %copy.13 = f32[512,64]{0,1:T(8,128)} copy(f32[512,64]{0,1:T(8,128)S(1)} %bitcast.9) | data formatting | bytes 262144
  52.4 0.1 copy-done.2
  52.4 1.1 %copy.14 = f32[5120,64]{0,1:T(8,128)} copy(f32[5120,64]{0,1:T(8,128)S(1)} %bitcast.13) | data formatting | bytes 2621440
Async XLA Ops:
  0.6 1.0 %copy-start = (f32[512,256]{1,0:T(8,128)S(1)}, f32[512,256]{1,0:T(8,128)}, u32[]{:S(2)}) copy-start(f32[512,256]{1,0:T(8,128)} %whitening.1) | copy-start | bytes 1572868
  1.7 0.9 %copy-start.1 = (f32[512,64]{0,1:T(8,128)S(1)}, f32[512,64]{0,1:T(8,128)}, u32[]{:S(2)}) copy-start(f32[512,64]{0,1:T(8,128)} %param.11) | copy-start | bytes 393220
  50.6 1.8 %copy-start.2 = (f32[64,5120]{1,0:T(8,128)S(1)}, f32[64,5120]{1,0:T(8,128)}, u32[]{:S(2)}) copy-start(f32[64,5120]{1,0:T(8,128)} %get-tuple-element.8) | copy-start | bytes 3932164
